TPU v7x, 32 devices: a whole 2x2x4 slice. The times are simulated.
32 devices in a mesh: runs: 2 (over y), grp: 4 (over x, core), mem: 4 (over z).
Axes of the slice: x: 2, y: 2, z: 4, core: 2. Of those that a mesh axis runs over, the one named last changes fastest.
Arguments:
- coords: float32 [256, 3, 512], P(('runs', 'grp', 'mem')), parts along dimension 0, may hold values from 0 to 128, as said below
- noise: float32 [256, 512], P(('runs', 'grp', 'mem')), parts along dimension 0, may hold values from 0.2 to 1
- right_side: float32 [256, 512], P(('runs', 'grp', 'mem')), parts along dimension 0, may hold values from -11 to 11
- tiles: int32 [256, 4, 2], P(('runs', 'grp', 'mem')), parts along dimension 0, may hold values from 0 to 127, as said below
- tile_count: int32 [256], P(('runs', 'grp', 'mem')), parts along dimension 0, may hold values from 1 to 4
Outputs:
- solution: float32 [256, 512], P(('runs', 'grp', 'mem')), parts along dimension 0
- residual: float32 [256, 512], P(('runs', 'grp', 'mem')), parts along dimension 0
There are 2 independent parts, one for each index of `runs`. A program takes and returns all parts, laid end to end along the dimension named above; each array names one. Nothing has to cross between parts.
Inputs may be any that keep to these rules, and one draw needn't show every extreme that they name: `tiles`: slot k < tile_count[r] of block row r holds (r, r + k); the remaining slots hold (r, r). Every block c >= r whose kernel tile with r is nonzero is listed. `coords`: the time coordinate of block b lies in [k, k + 1) for an integer time cell k of the block; every block lies wholly in one time cell, cells are nondecreasing along the blocks, and each cell holds 1 to 2 consecutive blocks.
All inputs are finite; a program needn't handle non-finite values.
Results may differ from a plain program's by a relative error of at most 0.0003.
Values sent between devices are 32-bit elements; how exact they have to be, the bound alone decides.
No kernel may reach another device: no remote copies, remote signals or barrier semaphores. Data moves between devices by JAX's collectives and lax.ppermute only.
A program may use at most 64 MiB of HBM per device.

v0:
```python
import functools

import jax
import jax.numpy as jnp
from jax import lax
from jax.experimental import pallas as pl
from jax.experimental.pallas import tpu as pltpu
from jax.sharding import PartitionSpec as P

SCALE = 0.2 * 16.0
TINY = 1e-30
LANES = 128
SUBLANES = 8
BAND = 128
UNROLL = 16
AXES = ("grp", "mem")
MIB = 1 << 20
X, Y, T, V, N, COUNT, ODD = range(7)
NEAR = 4.0
PARTS = ((0, 0), (0, 1), (1, 0), (1, 1), (0, 2), (2, 0))
NORM = 2 * len(PARTS)
ONES, TIMES, VECTOR = NORM + 3, NORM + 6, NORM + 9
FEATURES = 32

VMEM = pl.BlockSpec(memory_space=pltpu.VMEM)
SMEM = pl.BlockSpec(memory_space=pltpu.SMEM)
HBM = pl.BlockSpec(memory_space=pltpu.HBM)


def resident(*arrays):
    return [pltpu.with_memory_space_constraint(a, pltpu.VMEM) for a in arrays]


def call(kernel, out_shape, operands, specs, scratch=(), limit=8, aliases=None):
    return pl.pallas_call(
        kernel,
        out_shape=out_shape,
        in_specs=specs,
        out_specs=jax.tree.map(lambda _: VMEM, out_shape),
        scratch_shapes=list(scratch),
        input_output_aliases=aliases or {},
        compiler_params=pltpu.CompilerParams(vmem_limit_bytes=limit * MIB),
    )(*operands)


def shape(*dims):
    return jax.ShapeDtypeStruct(dims, jnp.float32)


def vmem(*dims, dtype=jnp.float32):
    return pltpu.VMEM(dims, dtype)


def entries(u, ti, tj, mode):
    u = jnp.maximum(u, TINY)
    s = u * lax.rsqrt(u)
    a = jnp.maximum(1.0 - s, 0.0)
    if mode == "same":
        d = jnp.abs(ti - tj)
        b = 1.0 - d
        f = d + 0.25
    else:
        b = jnp.maximum(ti - tj, 0.0)
        f = 1.25 - b
    p = a * b
    p = p * p
    return (p * p) * ((s + 0.25) * f)


def spread(row):
    return jnp.broadcast_to(row, (SUBLANES, row.shape[-1]))


def cut(ch):
    return slice(ch * LANES, (ch + 1) * LANES)


def block_at(c):
    return pl.ds(pl.multiple_of(c * SUBLANES, SUBLANES), SUBLANES)


def each_block(q, stride=SUBLANES):
    return pl.ds(q, SUBLANES, stride=stride)


def gather(rows, q):
    return jnp.concatenate([rows[ch, each_block(q), :] for ch in range(rows.shape[0])], axis=1)


def scatter(rows, at, z, first=0):
    for ch in range(z.shape[-1] // LANES):
        rows[first + ch, at, :] = z[:, cut(ch)]


def split(a):
    high = a.astype(jnp.bfloat16).astype(jnp.float32)
    rest = a - high
    middle = rest.astype(jnp.bfloat16).astype(jnp.float32)
    return [high, middle, rest - middle]


def left_features(x, y, t, v):
    xs, ys, one = split(x), split(y), jnp.ones_like(x)
    products = [xs[i] for i, _ in PARTS] + [ys[i] for i, _ in PARTS]
    return products + split(x * x + y * y) + [one] * 3 + split(t) + split(v)


def put_right(rt, wide, x, y):
    wide[...] = jnp.zeros_like(wide)
    xs, ys, one = split(x), split(y), jnp.ones_like(x)
    products = [-2.0 * xs[j] for _, j in PARTS] + [-2.0 * ys[j] for _, j in PARTS]
    for q, z in enumerate(products + [one] * 3 + split(x * x + y * y)):
        scatter(wide, each_block(q, FEATURES), z)
    for b in range(rt.shape[0]):
        for n in range(wide.shape[0]):
            rt[b, :, cut(n)] = wide[n, b * FEATURES : (b + 1) * FEATURES, :].astype(jnp.bfloat16)


def columns(lt, first, pairs):
    dims = (lt.shape[-1], LANES * pairs)
    row = lax.broadcasted_iota(jnp.int32, dims, 0) - first
    group = lax.broadcasted_iota(jnp.int32, dims, 1) // LANES
    pick = jnp.where((row >= 3 * group) & (row < 3 * group + 3), 1.0, 0.0)
    return jnp.dot(lt, pick.astype(jnp.bfloat16), preferred_element_type=jnp.float32)


def near(x, y):
    return jnp.max(jnp.maximum(jnp.abs(x), jnp.abs(y))) <= NEAR


def new_tile(fill, code, following, mode, diag, side, sign_of, k_ref, tcol, vcol, accl, accs, bufs):
    slot, r, c = code >> 8, (code >> 4) & 15, code & 15
    chunks = side.shape[0]
    bands = chunks * LANES // BAND
    sign = 1.0 if mode == "same" else sign_of(c)
    vj = [spread(side[ch, block_at(c), :][V : V + 1]) for ch in range(chunks)]
    tj = [sign * spread(side[ch, block_at(c), :][T : T + 1]) for ch in range(chunks)]
    zero = jnp.zeros((SUBLANES, LANES), jnp.float32)
    acc = [zero] * chunks
    for band in range(bands):
        first = band * BAND // LANES if diag else 0
        if band + 1 < bands:
            fill(bufs[(band + 1) % 2], r, c, band + 1, (band + 1) * BAND // LANES if diag else 0)
        else:
            fill(bufs[0], (following >> 4) & 15, following & 15, 0, 0)
        buf = bufs[band % 2]
        for g in range(BAND // SUBLANES):
            near_rows = slice(g * SUBLANES, (g + 1) * SUBLANES)
            at = slice(band * BAND + g * SUBLANES, band * BAND + (g + 1) * SUBLANES)
            ti = tcol[r, at, :]
            if mode == "next":
                ti = sign * ti + 1.0
            if accs is not None:
                vi = vcol[r, at, :]
            total = None
            for ch in range(first, chunks):
                m = entries(buf[near_rows, cut(ch)], ti, tj[ch], mode)
                k_ref[slot, at, cut(ch)] = m
                w = m * vj[ch]
                total = w if total is None else total + w
                if accs is not None and not (diag and ch == first):
                    acc[ch] = acc[ch] + m * vi
            accl[r, at, :] = total if diag else accl[r, at, :] + total
    if accs is not None:
        for ch in range(1 if diag else 0, chunks):
            accs[c, :, cut(ch)] += acc[ch]


def old_tile(code, row_of, k_ref, vcol, accl, accs, diag):
    slot, r, c = code >> 8, (code >> 4) & 15, code & 15
    width = k_ref.shape[-1]
    chunks = width // LANES
    vj = [spread(row_of(c, ch)) for ch in range(chunks)]
    zero = jnp.zeros((SUBLANES, LANES), jnp.float32)

    def rows_at(at, acc, used, single):
        acc = list(acc)
        if accs is not None:
            vi = vcol[r, at, :]
        total = None
        for q, ch in enumerate(used):
            m = k_ref[slot, at, cut(ch)]
            w = m * vj[ch]
            total = w if total is None else total + w
            if accs is not None and ch != single:
                acc[q] = acc[q] + m * vi
        accl[r, at, :] = total if diag else accl[r, at, :] + total
        return tuple(acc)

    def band(lo, hi, used, single):
        def step(it, acc):
            for g in range(UNROLL):
                start = pl.multiple_of((it * UNROLL + g) * SUBLANES, SUBLANES)
                acc = rows_at(pl.ds(start, SUBLANES), acc, used, single)
            return acc

        deep = SUBLANES * UNROLL
        acc = lax.fori_loop(lo // deep, hi // deep, step, tuple(zero for _ in used))
        if accs is not None:
            for q, ch in enumerate(used):
                if ch != single:
                    accs[c, :, cut(ch)] += acc[q]

    if diag:
        for ri in range(chunks):
            band(ri * LANES, (ri + 1) * LANES, list(range(ri, chunks)), ri)
    else:
        band(0, width, list(range(chunks)), -1)


def inner_slots(blocks, reach):
    return sum(blocks - k for k in range(reach + 1))


def list_inner(blocks, reach, count, todo, same):
    for r in range(blocks):
        todo[r] = (r << 8) | (r << 4) | r
    at = jnp.int32(blocks)
    ends = [at]

    def put(at, r, k, base, keep):
        todo[at] = ((base + r) << 8) | (r << 4) | (r + k)
        return at + keep.astype(jnp.int32)

    def bit(r):
        return ((same >> r) & 1) == 1

    at = lax.fori_loop(0, blocks - 1, lambda r, at: put(at, r, 1, 0, (count[r] > 1) & bit(r)), at)
    ends.append(at)
    at = lax.fori_loop(0, blocks - 1, lambda r, at: put(at, r, 1, 0, (count[r] > 1) & ~bit(r)), at)
    ends.append(at)
    base = 0
    for k in range(2, reach + 1):
        at = lax.fori_loop(0, blocks - k, lambda r, at, k=k, base=base: put(at, r, k, base, count[r] > k), at)
        base += blocks - k
    todo[at] = 0
    return ends + [at]


def list_outer(blocks, reach, count, low_count, todo, same):
    tiles = []
    slot = 0
    for k in range(1, reach + 1):
        for j in range(k):
            c, r = reach - k + j, blocks - k + j
            tiles.append((k, 0, (slot << 8) | (j << 4) | c, ((low_count >> (3 * c)) & 7) > k))
            tiles.append((k, 1, ((slot + 1) << 8) | (r << 4) | (reach + j), count[r] > k))
            slot += 2
    at = jnp.int32(0)
    ends = []
    for wanted in (True, False):
        for k, which, code, keep in tiles:
            together = ((same >> which) & 1) == 1 if k == 1 else None
            if wanted and k > 1:
                continue
            if k == 1:
                keep = keep & (together if wanted else ~together)
            todo[at] = code
            at += keep.astype(jnp.int32)
        ends.append(at)
    todo[at] = 0
    return ends


def cell(rows, b):
    at = b * SUBLANES + T
    return jnp.floor(rows[0, at : at + 1, 0:1])


def as_scalar(value):
    return jnp.max(jnp.broadcast_to(value, (1, LANES))).astype(jnp.int32)


def flag(condition, weight):
    return jnp.where(condition, float(weight), 0.0)


def low_counts(low):
    total = jnp.zeros((1, 1), jnp.float32)
    for b in range(low.shape[1] // SUBLANES):
        at = b * SUBLANES + COUNT
        total += low[0, at : at + 1, 0:1] * float(8**b)
    return total


def pack_kernel(count_in, coords_in, vector_in, noise_in, even_out, odd_out, packed, count, coords, vector, noise, sems):
    chunks = packed.shape[0]
    edge = even_out.shape[1]
    odd = lax.rem(position(), 2).astype(jnp.float32)
    copies = [
        pltpu.make_async_copy(source, target, sems.at[n])
        for n, (source, target) in enumerate(
            [(count_in, count), (coords_in, coords), (vector_in, vector), (noise_in, noise)]
        )
    ]
    for copy in copies:
        copy.start()
    for copy in copies:
        copy.wait()
    for q in (X, Y, T):
        scatter(packed, each_block(q), coords[q])
    scatter(packed, each_block(V), vector[...])
    scatter(packed, each_block(N), noise[...])
    for b in range(vector.shape[0]):
        at = b * SUBLANES + COUNT
        packed[:, at : at + 1, :] = jnp.full((chunks, 1, LANES), count[b].astype(jnp.float32))
        packed[:, at + 1 : (b + 1) * SUBLANES, :] = jnp.full((chunks, SUBLANES - ODD, LANES), odd)
    first, last = packed[:, 0:edge, :], packed[:, packed.shape[1] - edge :, :]
    even_out[...], odd_out[...] = by_parity(packed, last, first)


def centre(packed):
    head = packed[0, 0:SUBLANES, :]
    mean = jnp.sum(head, axis=1, keepdims=True) * (1.0 / LANES)
    return mean[X : X + 1], mean[Y : Y + 1], cell(packed, 0)


def matmul_fill(lt, rt):
    def fill(buf, r, c, band, first):
        own = lt[r, band * BAND : (band + 1) * BAND, :]
        at = slice(first * LANES, buf.shape[-1])
        buf[:, at] = jnp.dot(own, rt[c, :, at], preferred_element_type=jnp.float32)

    return fill


def difference_fill(packed, raw):
    def fill(buf, r, c, band, first):
        own = packed[band * BAND // LANES, block_at(r), :].T
        for ch in range(first, raw.shape[0]):
            other = raw[ch, block_at(c), :]
            dx, dy = [own[:, q : q + 1] - other[q : q + 1, :] for q in (X, Y)]
            buf[:, cut(ch)] = dx * dx + dy * dy

    return fill


def run_tiles(fill, todo, ends, modes, tile):
    code = todo[0]
    fill((code >> 4) & 15, code & 15)
    begin = 0
    for end, mode in zip(ends, modes):

        def body(n, _, mode=mode):
            tile(todo[n], todo[n + 1], mode)
            return 0

        lax.fori_loop(begin, end, body, 0)
        begin = end


def inner_kernel(
    reach, count, packed, k_same, k_next, k_far, tcol, lt, accl, accs, rows, vcol, flat, wide, rt, buf_a, buf_b, todo
):
    blocks = accs.shape[0]
    cx, cy, start = centre(packed)
    x, y = gather(packed, X) - cx, gather(packed, Y) - cy
    t, v = gather(packed, T) - start, gather(packed, V)
    flat[...] = jnp.zeros_like(flat)
    for q, z in enumerate(left_features(x, y, t, v)):
        scatter(flat, each_block(q, FEATURES), z)
    put_right(rt, wide, x, y)
    scatter(rows, each_block(T), t)
    scatter(rows, each_block(V), v)
    for b in range(blocks):
        for ch in range(flat.shape[0]):
            part = flat[ch, b * FEATURES : (b + 1) * FEATURES, :].T
            lt[b, cut(ch), :] = part.astype(jnp.bfloat16)
        both = columns(lt[b], TIMES, 2)
        tcol[b] = both[:, :LANES]
        vcol[b] = both[:, LANES:]
    accs[...] = jnp.zeros_like(accs)
    same = jnp.zeros((1, 1), jnp.float32)
    for r in range(blocks - 1):
        same += flag(cell(packed, r) == cell(packed, r + 1), 1 << r)
    ends = list_inner(blocks, reach, count, todo, as_scalar(same))
    bufs = (buf_a, buf_b)
    kinds = (("same", k_same), ("same", k_next), ("next", k_next), ("next", k_far))

    def run(fill):
        def tile(code, following, kind):
            mode, k_ref = kind
            new_tile(
                fill, code, following, mode, k_ref is k_same,
                rows, lambda c: 1.0, k_ref, tcol, vcol, accl, accs, bufs,
            )

        run_tiles(lambda r, c: fill(buf_a, r, c, 0, 0), todo, ends, kinds, tile)

    fast = near(x, y)
    pl.when(fast)(lambda: run(matmul_fill(lt, rt)))
    pl.when(jnp.logical_not(fast))(lambda: run(difference_fill(packed, packed)))


def outer_kernel(
    reach, count, with_even, with_odd, packed, tcol, lt, accl_in, accs,
    k_ref, image, even_out, odd_out, accl, listed, raw, rows, wide, rt, buf_a, buf_b, todo,
):
    blocks = accs.shape[0]
    edge = reach * SUBLANES
    cx, cy, start = centre(packed)
    raw[...] = jnp.zeros_like(raw)
    high, low = by_parity(packed, with_even[...], with_odd[...])
    raw[:, 0:edge, :] = low
    raw[:, edge : 2 * edge, :] = high
    x, y = gather(raw, X) - cx, gather(raw, Y) - cy
    t = gather(raw, T) - start
    place = lax.broadcasted_iota(jnp.int32, (SUBLANES, 1), 0)
    put_right(rt, wide, x, y)
    scatter(rows, each_block(T), t)
    scatter(rows, each_block(V), gather(raw, V))
    scalars = low_counts(low)
    listed[...] = jnp.broadcast_to(scalars, listed.shape)
    scalars += flag(cell(low, reach - 1) == cell(packed, 0), 1 << (3 * reach))
    scalars += flag(cell(packed, blocks - 1) == cell(high, 0), 1 << (3 * reach + 1))
    code = as_scalar(scalars)
    ends = list_outer(blocks, reach, count, code, todo, code >> (3 * reach))
    bufs = (buf_a, buf_b)

    def run(fill):
        def tile(code, following, mode):
            new_tile(
                fill, code, following, mode, False,
                rows, lambda c: jnp.where(c < reach, -1.0, 1.0), k_ref, tcol, None, accl, None, bufs,
            )

        run_tiles(lambda r, c: fill(buf_a, r, c, 0, 0), todo, ends, ("same", "next"), tile)

    halo = jnp.where(place < 2 * reach, 1.0, 0.0)
    own_x, own_y = gather(packed, X) - cx, gather(packed, Y) - cy
    reach_x = jnp.maximum(jnp.abs(x * halo), jnp.abs(own_x))
    reach_y = jnp.maximum(jnp.abs(y * halo), jnp.abs(own_y))
    fast = near(reach_x, reach_y)
    pl.when(fast)(lambda: run(matmul_fill(lt, rt)))
    pl.when(jnp.logical_not(fast))(lambda: run(difference_fill(packed, raw)))
    summed = jnp.sum(accs[...], axis=1) + jnp.sum(accl[...], axis=-1)
    image[...] = gather(packed, N) * gather(packed, V) + SCALE * summed
    even_out[...], odd_out[...] = by_parity(packed, image[blocks - reach :, :], image[0:reach, :])


def again_kernel(reach, count, image, k_same, k_next, k_far, accl, accs, rows, vcol, flat, todo):
    blocks, width = image.shape
    flat[...] = jnp.zeros_like(flat)
    for n, part in enumerate(split(image[...])):
        scatter(flat, pl.ds(n, blocks, stride=3), part)
    lt = jnp.concatenate([flat[ch].T for ch in range(flat.shape[0])], axis=0).astype(jnp.bfloat16)
    for b in range(blocks):
        rows[b, 0:1, :] = image[b : b + 1, :]
    for b in range(0, blocks, 2):
        both = columns(lt, 3 * b, 2)
        vcol[b] = both[:, :LANES]
        vcol[b + 1] = both[:, LANES:]
    accs[...] = jnp.zeros_like(accs)
    ends = list_inner(blocks, reach, count, todo, jnp.int32(0))

    def row_of(c, ch):
        return rows[c, 0:1, cut(ch)]

    for begin, end, k_ref in ((0, ends[0], k_same), (ends[0], ends[2], k_next), (ends[2], ends[3], k_far)):

        def body(n, _, k_ref=k_ref):
            old_tile(todo[n], row_of, k_ref, vcol, accl, accs, k_ref is k_same)
            return 0

        lax.fori_loop(begin, end, body, 0)


def dots(pairs):
    lane = lax.broadcasted_iota(jnp.int32, (1, LANES), 1)
    out = jnp.zeros((1, LANES), jnp.float32)
    for n, (a, b) in enumerate(pairs):
        total = jnp.sum(jnp.sum(a * b, axis=1, keepdims=True), axis=0, keepdims=True)
        out = jnp.where(lane == n, total, out)
    return out


def close_kernel(
    reach, count, with_even, with_odd, listed, packed, image, k_ref, accl_in, accs, again, sums, accl, rows, todo
):
    blocks = image.shape[0]
    high, low = by_parity(packed, with_even[...], with_odd[...])
    for b in range(reach):
        rows[b, 0:1, :] = low[b : b + 1, :]
        rows[reach + b, 0:1, :] = high[b : b + 1, :]
    ends = list_outer(blocks, reach, count, as_scalar(listed[0:1, :]), todo, jnp.int32(0))

    def body(n, _):
        old_tile(todo[n], lambda c, ch: rows[c, 0:1, cut(ch)], k_ref, None, accl, None, False)
        return 0

    lax.fori_loop(0, ends[-1], body, 0)
    summed = jnp.sum(accs[...], axis=1) + jnp.sum(accl[...], axis=-1)
    q = image[...]
    p = gather(packed, N) * q + SCALE * summed
    again[...] = p
    b = gather(packed, V)
    sums[...] = jnp.broadcast_to(dots([(b, b), (b, q), (q, q), (b, p), (q, p)]), sums.shape)


def finish_kernel(sums, packed, image, again, solution, residual):
    total = jnp.sum(sums[...], axis=0, keepdims=True)
    bb, bq, qq, bp, qp = [total[:, n : n + 1] for n in range(5)]
    alpha = bb / bq
    rq = bq - alpha * qq
    rr = (bb - alpha * bq) - alpha * rq
    beta = rr / bb
    r_ar = rq - alpha * (bp - alpha * qp)
    b_ar = bq - alpha * bp
    curvature = r_ar + beta * (rq + b_ar) + beta * beta * bq
    gamma = rr / curvature
    b, q, p = gather(packed, V), image[...], again[...]
    r = b - alpha * q
    d = r + beta * b
    ad = (q - alpha * p) + beta * q
    solution[...] = alpha * b + gamma * d
    residual[...] = r - gamma * ad


def position():
    place = 0
    for axis in AXES:
        place = place * lax.axis_size(axis) + lax.axis_index(axis)
    return place


def by_parity(packed, low, high):
    odd = packed[0, ODD : ODD + 1, 0:1] > 0.5
    return jnp.where(odd, high, low), jnp.where(odd, low, high)


def swap(value, start):
    pairs = [(i, i + 1) for i in range(start, lax.axis_size(AXES) - 1, 2)]
    return lax.ppermute(value, AXES, pairs + [(b, a) for a, b in pairs])


def local(coords, noise, right_side, tiles, tile_count):
    blocks, width = right_side.shape
    reach = tiles.shape[1] - 1
    chunks = width // LANES
    edge = (chunks, reach * SUBLANES, LANES)
    half = jnp.bfloat16
    inner = inner_slots(blocks, reach) - blocks
    bands = [vmem(BAND, width), vmem(BAND, width)]
    factors = [vmem(chunks, SUBLANES * FEATURES, LANES), vmem(SUBLANES, FEATURES, width, dtype=half)]
    rows = vmem(chunks, SUBLANES * SUBLANES, LANES)
    todo = pltpu.SMEM((inner + blocks + 2,), jnp.int32)

    operands = (tile_count, jnp.transpose(coords, (1, 0, 2)), right_side, noise)
    even_out, odd_out, packed = call(
        pack_kernel,
        (shape(*edge), shape(*edge), vmem(chunks, blocks * SUBLANES, LANES)),
        [pltpu.with_memory_space_constraint(a, pltpu.HBM) for a in operands],
        [HBM] * 4,
        [
            pltpu.SMEM((blocks,), jnp.int32),
            vmem(3, blocks, width),
            vmem(blocks, width),
            vmem(blocks, width),
            pltpu.SemaphoreType.DMA((4,)),
        ],
    )
    with_even, with_odd = swap(even_out, 0), swap(odd_out, 1)
    (packed,) = resident(packed)
    *k_in, tcol, lt, accl, accs = call(
        functools.partial(inner_kernel, reach),
        (
            vmem(blocks, width, width),
            vmem(blocks - 1, width, width),
            vmem(inner - blocks + 1, width, width),
            vmem(blocks, width, LANES),
            vmem(blocks, width, FEATURES, dtype=half),
            vmem(blocks, width, LANES),
            vmem(blocks, SUBLANES, width),
        ),
        (tile_count, packed),
        [SMEM, VMEM],
        [rows, vmem(blocks, width, LANES), vmem(chunks, blocks * FEATURES, LANES), *factors, *bands, todo],
    )
    *k_in, tcol, lt, accl, accs = resident(*k_in, tcol, lt, accl, accs)
    k_out, image, even_out, odd_out, accl, listed = call(
        functools.partial(outer_kernel, reach),
        (
            vmem(reach * (reach + 1), width, width),
            vmem(blocks, width),
            shape(reach, width),
            shape(reach, width),
            vmem(blocks, width, LANES),
            vmem(SUBLANES, LANES),
        ),
        (tile_count, with_even, with_odd, packed, tcol, lt, accl, accs),
        [SMEM] + [VMEM] * 7,
        [rows, rows, *factors, *bands, todo],
        aliases={6: 4},
    )
    with_even, with_odd = swap(even_out, 0), swap(odd_out, 1)
    image, *k_in = resident(image, *k_in)
    accl, accs = call(
        functools.partial(again_kernel, reach),
        (vmem(blocks, width, LANES), vmem(blocks, SUBLANES, width)),
        (tile_count, image, *k_in),
        [SMEM] + [VMEM] * 4,
        [vmem(blocks, SUBLANES, width), vmem(blocks, width, LANES), vmem(chunks, LANES, LANES), todo],
    )
    k_out, accl, accs, listed = resident(k_out, accl, accs, listed)
    devices = lax.axis_size(AXES)
    again, sums, _ = call(
        functools.partial(close_kernel, reach),
        (vmem(blocks, width), shape(devices, LANES), vmem(blocks, width, LANES)),
        (tile_count, with_even, with_odd, listed, packed, image, k_out, accl, accs),
        [SMEM] + [VMEM] * 8,
        [vmem(2 * reach, SUBLANES, width), todo],
        aliases={7: 2},
    )
    sums = lax.all_to_all(sums, AXES, 0, 0, tiled=True)
    (again,) = resident(again)
    return call(
        finish_kernel,
        (shape(blocks, width), shape(blocks, width)),
        (sums, packed, image, again),
        [VMEM] * 4,
    )


def solution(mesh):
    in_specs = (
        P(("runs", "grp", "mem"), None, None),
        P(("runs", "grp", "mem"), None),
        P(("runs", "grp", "mem"), None),
        P(("runs", "grp", "mem"), None, None),
        P(("runs", "grp", "mem")),
    )
    out_specs = (P(("runs", "grp", "mem"), None), P(("runs", "grp", "mem"), None))
    return jax.shard_map(local, mesh=mesh, in_specs=in_specs, out_specs=out_specs, check_vma=False)
```

profile of v0, /device:TPU:0, one launch (start us, length us, event | category | flops | bytes accessed | tf_op | source)
XLA Modules:
  0.0 55.5 jit_solution(6999796042370707320)
XLA Ops:
  0.6 0.9 %shard_map.59 = (f32[4,24,128]{2,1,0:T(8,128)S(1)}, f32[4,24,128]{2,1,0:T(8,128)S(1)}, f32[4,64,128]{2,1,0:T(8,128)S(1)}) custom-call(s32[8]{0:T(128)} %count.7, f32[3,8,512]{2,1,0:T(8,128)} %bitcast.7, f32[8,512]{1,0:T(8,128)} %vector_in.1, f32[8,512]{1,0:T(8,128)} %noise_in.1), custom_call_target="tpu_custom_call" | custom-call | tf_op jit(solution)/shard_map/pallas_call | solution.py:35
  1.5 3.1 %collective-permute-start = (f32[4,24,128]{2,1,0:T(8,128)S(1)}, f32[4,24,128]{2,1,0:T(8,128)S(1)}, u32[]{:S(2)}, u32[]{:S(2)}) collective-permute-start(f32[4,24,128]{2,1,0:T(8,128)S(1)} %get-tuple-element.21), channel_id=1, source_target_pairs={{0,1},{2,3},{4,5},{6,7},{8,9},{10,11},{12,13},{14,15},{1,0},{3,2},... | collective-permute-start | bytes 147464 | tf_op jit(solution)/shard_map/ppermute | solution.py:533
  4.6 0.7 %collective-permute-start.1 = (f32[4,24,128]{2,1,0:T(8,128)S(1)}, f32[4,24,128]{2,1,0:T(8,128)S(1)}, u32[]{:S(2)}, u32[]{:S(2)}) collective-permute-start(f32[4,24,128]{2,1,0:T(8,128)S(1)} %get-tuple-element.22), channel_id=1, source_target_pairs={{1,2},{3,4},{5,6},{7,8},{9,10},{11,12},{13,14},{2,1},{4,3},{6,5},{... | collective-permute-start | bytes 147464 | tf_op jit(solution)/shard_map/ppermute | solution.py:533
  5.3 0.0 copy-start
  5.3 0.6 %copy-done = s32[8]{0:T(128)S(1)} copy-done((s32[8]{0:T(128)S(1)}, s32[8]{0:T(128)}, u32[]{:S(2)}) %copy-start) | copy-done | bytes 56
  6.0 15.7 %shard_map.60 = (f32[8,512,512]{2,1,0:T(8,128)S(1)}, f32[7,512,512]{2,1,0:T(8,128)S(1)}, f32[11,512,512]{2,1,0:T(8,128)S(1)}, f32[8,512,128]{2,1,0:T(8,128)S(1)}...) custom-call(s32[8]{0:T(128)S(1)} %copy-done, ...), custom_call_target="tpu_custom_call" | custom-call | tf_op jit(solution)/shard_map/pallas_call | solution.py:35
  21.7 0.0 collective-permute-done.with_even
  21.7 0.0 collective-permute-done.1.with_odd
  21.7 4.6 %shard_map.61 = (f32[12,512,512]{2,1,0:T(8,128)S(1)}, f32[8,512]{1,0:T(8,128)S(1)}, f32[3,512]{1,0:T(4,128)S(1)}, f32[3,512]{1,0:T(4,128)S(1)}, f32[8,512,128]{2,1,0:T(8,128)S(1)}, /*index=5*/f32[8,128]{1,0:T(8,128)S(1)}) custom-call(s32[8]{0:T(128)S(1)} %copy-done, ...), custom_call_target="tpu_custom_call", output_to_operand_aliasing={{4}: (6, {})} | custom-call | tf_op jit(solution)/shard_map/pallas_call | solution.py:35
  26.3 3.7 %collective-permute-start.2 = (f32[3,512]{1,0:T(4,128)S(1)}, f32[3,512]{1,0:T(4,128)S(1)}, u32[]{:S(2)}, u32[]{:S(2)}) collective-permute-start(f32[3,512]{1,0:T(4,128)S(1)} %get-tuple-element.28), channel_id=1, source_target_pairs={{0,1},{2,3},{4,5},{6,7},{8,9},{10,11},{12,13},{14,15},{1,0},{3,2},... | collective-permute-start | bytes 18440 | tf_op jit(solution)/shard_map/ppermute | solution.py:533
  30.0 0.6 %collective-permute-start.3 = (f32[3,512]{1,0:T(4,128)S(1)}, f32[3,512]{1,0:T(4,128)S(1)}, u32[]{:S(2)}, u32[]{:S(2)}) collective-permute-start(f32[3,512]{1,0:T(4,128)S(1)} %get-tuple-element.29), channel_id=1, source_target_pairs={{1,2},{3,4},{5,6},{7,8},{9,10},{11,12},{13,14},{2,1},{4,3},{6,5},{... | collective-permute-start | bytes 18440 | tf_op jit(solution)/shard_map/ppermute | solution.py:533
  30.6 4.0 %shard_map.62 = (f32[8,512,128]{2,1,0:T(8,128)S(1)}, f32[8,8,512]{2,1,0:T(8,128)S(1)}) custom-call(s32[8]{0:T(128)S(1)} %copy-done, f32[8,512]{1,0:T(8,128)S(1)} %get-tuple-element.31.image, f32[8,512,512]{2,1,0:T(8,128)S(1)} %get-tuple-element.33.k_same, f32[7,512,512]{2,1,0:T(8,128)S(1)} %get-tuple-element.34.k_next, ...), custom_call_target="tpu_custom_call" | custom-call | tf_op jit(solution)/shard_map/pallas_call | solution.py:35
  34.6 0.0 collective-permute-done.2.with_even
  34.6 0.0 collective-permute-done.3.with_odd
  34.6 2.0 %shard_map.63 = (f32[8,512]{1,0:T(8,128)S(1)}, f32[16,128]{1,0:T(8,128)S(1)}, f32[8,512,128]{2,1,0:T(8,128)S(1)}) custom-call(s32[8]{0:T(128)S(1)} %copy-done, f32[3,512]{1,0:T(4,128)S(1)} %collective-permute-done.2.with_even, f32[3,512]{1,0:T(4,128)S(1)} %collective-permute-done.3.with_odd, ...), custom_call_target="tpu_custom_call", output_to_operand_aliasing={{2}: (7, {})} | custom-call | tf_op jit(solution)/shard_map/pallas_call | solution.py:35
  36.6 17.9 %all_to_all.11 = f32[16,1,128]{2,1,0:T(1,128)S(1)} all-to-all(f32[16,1,128]{2,1,0:T(1,128)S(1)} %bitcast.6), channel_id=1, replica_groups=mesh['runs'=2,'grp'=4,'mem'=4] {'grp','mem'}, dimensions={0} | all-to-all | bytes 16384 | tf_op jit(solution)/shard_map/all_to_all | solution.py:614
  54.5 1.0 %shard_map.64 = (f32[8,512]{1,0:T(8,128)}, f32[8,512]{1,0:T(8,128)}) custom-call(f32[16,128]{1,0:T(8,128)S(1)} %bitcast.5, f32[4,64,128]{2,1,0:T(8,128)S(1)} %get-tuple-element.23.packed, f32[8,512]{1,0:T(8,128)S(1)} %get-tuple-element.31.image, f32[8,512]{1,0:T(8,128)S(1)} %get-tuple-element.39.again), custom_call_target="tpu_custom_call" | custom-call | tf_op jit(solution)/shard_map/pallas_call | solution.py:35
Async XLA Ops:
  1.5 20.2 %collective-permute-start = (f32[4,24,128]{2,1,0:T(8,128)S(1)}, f32[4,24,128]{2,1,0:T(8,128)S(1)}, u32[]{:S(2)}, u32[]{:S(2)}) collective-permute-start(f32[4,24,128]{2,1,0:T(8,128)S(1)} %get-tuple-element.21), channel_id=1, source_target_pairs={{0,1},{2,3},{4,5},{6,7},{8,9},{10,11},{12,13},{14,15},{1,0},{3,2},... | collective-permute-start | bytes 147464 | tf_op jit(solution)/shard_map/ppermute | solution.py:533
  4.6 17.1 %collective-permute-start.1 = (f32[4,24,128]{2,1,0:T(8,128)S(1)}, f32[4,24,128]{2,1,0:T(8,128)S(1)}, u32[]{:S(2)}, u32[]{:S(2)}) collective-permute-start(f32[4,24,128]{2,1,0:T(8,128)S(1)} %get-tuple-element.22), channel_id=1, source_target_pairs={{1,2},{3,4},{5,6},{7,8},{9,10},{11,12},{13,14},{2,1},{4,3},{6,5},{... | collective-permute-start | bytes 147464 | tf_op jit(solution)/shard_map/ppermute | solution.py:533
  5.3 0.7 %copy-start = (s32[8]{0:T(128)S(1)}, s32[8]{0:T(128)}, u32[]{:S(2)}) copy-start(s32[8]{0:T(128)} %count.7) | copy-start | bytes 100
  26.3 8.3 %collective-permute-start.2 = (f32[3,512]{1,0:T(4,128)S(1)}, f32[3,512]{1,0:T(4,128)S(1)}, u32[]{:S(2)}, u32[]{:S(2)}) collective-permute-start(f32[3,512]{1,0:T(4,128)S(1)} %get-tuple-element.28), channel_id=1, source_target_pairs={{0,1},{2,3},{4,5},{6,7},{8,9},{10,11},{12,13},{14,15},{1,0},{3,2},... | collective-permute-start | bytes 18440 | tf_op jit(solution)/shard_map/ppermute | solution.py:533
  30.0 4.6 %collective-permute-start.3 = (f32[3,512]{1,0:T(4,128)S(1)}, f32[3,512]{1,0:T(4,128)S(1)}, u32[]{:S(2)}, u32[]{:S(2)}) collective-permute-start(f32[3,512]{1,0:T(4,128)S(1)} %get-tuple-element.29), channel_id=1, source_target_pairs={{1,2},{3,4},{5,6},{7,8},{9,10},{11,12},{13,14},{2,1},{4,3},{6,5},{... | collective-permute-start | bytes 18440 | tf_op jit(solution)/shard_map/ppermute | solution.py:533
where the time goes:
time: 55.4 us; the launch traced here: 55.5 us
  Pallas kernels  28.2 us (51%)
  blocking collectives  17.9 us (32%)
  starting transfers between devices  8.04 us (15%)
  between operations  0.71 us (1%)
  local copies, waits for them, and re-layouts  0.65 us (1%)
    pallas_call x6, Pallas kernels, call(): pl.pallas_call(kernel, out_shape=out_shape, in_specs=specs, out_specs=jax...  28.2 us
    all_to_all x1, blocking collectives, local(): sums = lax.all_to_all(sums, AXES, 0, 0, tiled=True)  17.9 us
    ppermute x4, starting transfers between devices, swap(): return lax.ppermute(value, AXES, pairs + [(b, a) for a, b in pairs])  8.04 us
  transfers between devices with their start and end apart: 4, of which 0 were waited for; matrix products, arithmetic and copies ran while one was open for 0% of the time, Pallas kernels for 35%

commit v1 on v0

--- a/solution.py
+++ b/solution.py
@@ -23,7 +23,6 @@
 FEATURES = 32
 
 VMEM = pl.BlockSpec(memory_space=pltpu.VMEM)
-SMEM = pl.BlockSpec(memory_space=pltpu.SMEM)
 HBM = pl.BlockSpec(memory_space=pltpu.HBM)
 
 
@@ -52,7 +51,6 @@
 
 
 def entries(u, ti, tj, mode):
-    u = jnp.maximum(u, TINY)
     s = u * lax.rsqrt(u)
     a = jnp.maximum(1.0 - s, 0.0)
     if mode == "same":
@@ -212,6 +210,21 @@
     return sum(blocks - k for k in range(reach + 1))
 
 
+def with_counts(kernel):
+    def run(reach, counts, *refs):
+        *refs, held, sem = refs
+        copy = pltpu.make_async_copy(counts.at[0:1, :], held, sem)
+        copy.start()
+
+        def ready():
+            copy.wait()
+            return lambda r: held[0, r]
+
+        kernel(reach, ready, *refs)
+
+    return run
+
+
 def list_inner(blocks, reach, count, todo, same):
     for r in range(blocks):
         todo[r] = (r << 8) | (r << 4) | r
@@ -225,13 +238,13 @@
     def bit(r):
         return ((same >> r) & 1) == 1
 
-    at = lax.fori_loop(0, blocks - 1, lambda r, at: put(at, r, 1, 0, (count[r] > 1) & bit(r)), at)
+    at = lax.fori_loop(0, blocks - 1, lambda r, at: put(at, r, 1, 0, (count(r) > 1) & bit(r)), at)
     ends.append(at)
-    at = lax.fori_loop(0, blocks - 1, lambda r, at: put(at, r, 1, 0, (count[r] > 1) & ~bit(r)), at)
+    at = lax.fori_loop(0, blocks - 1, lambda r, at: put(at, r, 1, 0, (count(r) > 1) & ~bit(r)), at)
     ends.append(at)
     base = 0
     for k in range(2, reach + 1):
-        at = lax.fori_loop(0, blocks - k, lambda r, at, k=k, base=base: put(at, r, k, base, count[r] > k), at)
+        at = lax.fori_loop(0, blocks - k, lambda r, at, k=k, base=base: put(at, r, k, base, count(r) > k), at)
         base += blocks - k
     todo[at] = 0
     return ends + [at]
@@ -244,7 +257,7 @@
         for j in range(k):
             c, r = reach - k + j, blocks - k + j
             tiles.append((k, 0, (slot << 8) | (j << 4) | c, ((low_count >> (3 * c)) & 7) > k))
-            tiles.append((k, 1, ((slot + 1) << 8) | (r << 4) | (reach + j), count[r] > k))
+            tiles.append((k, 1, ((slot + 1) << 8) | (r << 4) | (reach + j), count(r) > k))
             slot += 2
     at = jnp.int32(0)
     ends = []
@@ -283,7 +296,7 @@
     return total
 
 
-def pack_kernel(count_in, coords_in, vector_in, noise_in, even_out, odd_out, packed, count, coords, vector, noise, sems):
+def pack_kernel(count_in, coords_in, vector_in, noise_in, even_out, odd_out, packed, counts, count, coords, vector, noise, sems):
     chunks = packed.shape[0]
     edge = even_out.shape[1]
     odd = lax.rem(position(), 2).astype(jnp.float32)
@@ -301,10 +314,14 @@
         scatter(packed, each_block(q), coords[q])
     scatter(packed, each_block(V), vector[...])
     scatter(packed, each_block(N), noise[...])
+    lane = lax.broadcasted_iota(jnp.int32, (1, LANES), 1)
+    row = jnp.zeros((1, LANES), jnp.int32)
     for b in range(vector.shape[0]):
+        row = jnp.where(lane == b, count[b], row)
         at = b * SUBLANES + COUNT
         packed[:, at : at + 1, :] = jnp.full((chunks, 1, LANES), count[b].astype(jnp.float32))
         packed[:, at + 1 : (b + 1) * SUBLANES, :] = jnp.full((chunks, SUBLANES - ODD, LANES), odd)
+    counts[...] = jnp.broadcast_to(row, counts.shape)
     first, last = packed[:, 0:edge, :], packed[:, packed.shape[1] - edge :, :]
     even_out[...], odd_out[...] = by_parity(packed, last, first)
 
@@ -319,7 +336,8 @@
     def fill(buf, r, c, band, first):
         own = lt[r, band * BAND : (band + 1) * BAND, :]
         at = slice(first * LANES, buf.shape[-1])
-        buf[:, at] = jnp.dot(own, rt[c, :, at], preferred_element_type=jnp.float32)
+        u = jnp.dot(own, rt[c, :, at], preferred_element_type=jnp.float32)
+        buf[:, at] = jnp.maximum(u, TINY)
 
     return fill
 
@@ -330,7 +348,7 @@
         for ch in range(first, raw.shape[0]):
             other = raw[ch, block_at(c), :]
             dx, dy = [own[:, q : q + 1] - other[q : q + 1, :] for q in (X, Y)]
-            buf[:, cut(ch)] = dx * dx + dy * dy
+            buf[:, cut(ch)] = jnp.maximum(dx * dx + dy * dy, TINY)
 
     return fill
 
@@ -350,7 +368,7 @@
 
 
 def inner_kernel(
-    reach, count, packed, k_same, k_next, k_far, tcol, lt, accl, accs, rows, vcol, flat, wide, rt, buf_a, buf_b, todo
+    reach, ready, packed, k_same, k_next, k_far, tcol, lt, accl, accs, rows, vcol, flat, wide, rt, buf_a, buf_b, todo
 ):
     blocks = accs.shape[0]
     cx, cy, start = centre(packed)
@@ -373,7 +391,7 @@
     same = jnp.zeros((1, 1), jnp.float32)
     for r in range(blocks - 1):
         same += flag(cell(packed, r) == cell(packed, r + 1), 1 << r)
-    ends = list_inner(blocks, reach, count, todo, as_scalar(same))
+    ends = list_inner(blocks, reach, ready(), todo, as_scalar(same))
     bufs = (buf_a, buf_b)
     kinds = (("same", k_same), ("same", k_next), ("next", k_next), ("next", k_far))
 
@@ -393,7 +411,7 @@
 
 
 def outer_kernel(
-    reach, count, with_even, with_odd, packed, tcol, lt, accl_in, accs,
+    reach, ready, with_even, with_odd, packed, tcol, lt, accl_in, accs,
     k_ref, image, even_out, odd_out, accl, listed, raw, rows, wide, rt, buf_a, buf_b, todo,
 ):
     blocks = accs.shape[0]
@@ -414,7 +432,7 @@
     scalars += flag(cell(low, reach - 1) == cell(packed, 0), 1 << (3 * reach))
     scalars += flag(cell(packed, blocks - 1) == cell(high, 0), 1 << (3 * reach + 1))
     code = as_scalar(scalars)
-    ends = list_outer(blocks, reach, count, code, todo, code >> (3 * reach))
+    ends = list_outer(blocks, reach, ready(), code, todo, code >> (3 * reach))
     bufs = (buf_a, buf_b)
 
     def run(fill):
@@ -438,7 +456,7 @@
     even_out[...], odd_out[...] = by_parity(packed, image[blocks - reach :, :], image[0:reach, :])
 
 
-def again_kernel(reach, count, image, k_same, k_next, k_far, accl, accs, rows, vcol, flat, todo):
+def again_kernel(reach, ready, image, k_same, k_next, k_far, accl, accs, rows, vcol, flat, todo):
     blocks, width = image.shape
     flat[...] = jnp.zeros_like(flat)
     for n, part in enumerate(split(image[...])):
@@ -451,7 +469,7 @@
         vcol[b] = both[:, :LANES]
         vcol[b + 1] = both[:, LANES:]
     accs[...] = jnp.zeros_like(accs)
-    ends = list_inner(blocks, reach, count, todo, jnp.int32(0))
+    ends = list_inner(blocks, reach, ready(), todo, jnp.int32(0))
 
     def row_of(c, ch):
         return rows[c, 0:1, cut(ch)]
@@ -475,14 +493,14 @@
 
 
 def close_kernel(
-    reach, count, with_even, with_odd, listed, packed, image, k_ref, accl_in, accs, again, sums, accl, rows, todo
+    reach, ready, with_even, with_odd, listed, packed, image, k_ref, accl_in, accs, again, sums, accl, rows, todo
 ):
     blocks = image.shape[0]
     high, low = by_parity(packed, with_even[...], with_odd[...])
     for b in range(reach):
         rows[b, 0:1, :] = low[b : b + 1, :]
         rows[reach + b, 0:1, :] = high[b : b + 1, :]
-    ends = list_outer(blocks, reach, count, as_scalar(listed[0:1, :]), todo, jnp.int32(0))
+    ends = list_outer(blocks, reach, ready(), as_scalar(listed[0:1, :]), todo, jnp.int32(0))
 
     def body(n, _):
         old_tile(todo[n], lambda c, ch: rows[c, 0:1, cut(ch)], k_ref, None, accl, None, False)
@@ -544,11 +562,12 @@
     factors = [vmem(chunks, SUBLANES * FEATURES, LANES), vmem(SUBLANES, FEATURES, width, dtype=half)]
     rows = vmem(chunks, SUBLANES * SUBLANES, LANES)
     todo = pltpu.SMEM((inner + blocks + 2,), jnp.int32)
+    held = [pltpu.SMEM((1, LANES), jnp.int32), pltpu.SemaphoreType.DMA]
 
     operands = (tile_count, jnp.transpose(coords, (1, 0, 2)), right_side, noise)
-    even_out, odd_out, packed = call(
+    even_out, odd_out, packed, counts = call(
         pack_kernel,
-        (shape(*edge), shape(*edge), vmem(chunks, blocks * SUBLANES, LANES)),
+        (shape(*edge), shape(*edge), vmem(chunks, blocks * SUBLANES, LANES), vmem(SUBLANES, LANES, dtype=jnp.int32)),
         [pltpu.with_memory_space_constraint(a, pltpu.HBM) for a in operands],
         [HBM] * 4,
         [
@@ -560,9 +579,9 @@
         ],
     )
     with_even, with_odd = swap(even_out, 0), swap(odd_out, 1)
-    (packed,) = resident(packed)
+    packed, counts = resident(packed, counts)
     *k_in, tcol, lt, accl, accs = call(
-        functools.partial(inner_kernel, reach),
+        functools.partial(with_counts(inner_kernel), reach),
         (
             vmem(blocks, width, width),
             vmem(blocks - 1, width, width),
@@ -572,13 +591,13 @@
             vmem(blocks, width, LANES),
             vmem(blocks, SUBLANES, width),
         ),
-        (tile_count, packed),
-        [SMEM, VMEM],
-        [rows, vmem(blocks, width, LANES), vmem(chunks, blocks * FEATURES, LANES), *factors, *bands, todo],
+        (counts, packed),
+        [VMEM] * 2,
+        [rows, vmem(blocks, width, LANES), vmem(chunks, blocks * FEATURES, LANES), *factors, *bands, todo, *held],
     )
     *k_in, tcol, lt, accl, accs = resident(*k_in, tcol, lt, accl, accs)
     k_out, image, even_out, odd_out, accl, listed = call(
-        functools.partial(outer_kernel, reach),
+        functools.partial(with_counts(outer_kernel), reach),
         (
             vmem(reach * (reach + 1), width, width),
             vmem(blocks, width),
@@ -587,28 +606,28 @@
             vmem(blocks, width, LANES),
             vmem(SUBLANES, LANES),
         ),
-        (tile_count, with_even, with_odd, packed, tcol, lt, accl, accs),
-        [SMEM] + [VMEM] * 7,
-        [rows, rows, *factors, *bands, todo],
+        (counts, with_even, with_odd, packed, tcol, lt, accl, accs),
+        [VMEM] * 8,
+        [rows, rows, *factors, *bands, todo, *held],
         aliases={6: 4},
     )
     with_even, with_odd = swap(even_out, 0), swap(odd_out, 1)
     image, *k_in = resident(image, *k_in)
     accl, accs = call(
-        functools.partial(again_kernel, reach),
+        functools.partial(with_counts(again_kernel), reach),
         (vmem(blocks, width, LANES), vmem(blocks, SUBLANES, width)),
-        (tile_count, image, *k_in),
-        [SMEM] + [VMEM] * 4,
-        [vmem(blocks, SUBLANES, width), vmem(blocks, width, LANES), vmem(chunks, LANES, LANES), todo],
+        (counts, image, *k_in),
+        [VMEM] * 5,
+        [vmem(blocks, SUBLANES, width), vmem(blocks, width, LANES), vmem(chunks, LANES, LANES), todo, *held],
     )
     k_out, accl, accs, listed = resident(k_out, accl, accs, listed)
     devices = lax.axis_size(AXES)
     again, sums, _ = call(
-        functools.partial(close_kernel, reach),
+        functools.partial(with_counts(close_kernel), reach),
         (vmem(blocks, width), shape(devices, LANES), vmem(blocks, width, LANES)),
-        (tile_count, with_even, with_odd, listed, packed, image, k_out, accl, accs),
-        [SMEM] + [VMEM] * 8,
-        [vmem(2 * reach, SUBLANES, width), todo],
+        (counts, with_even, with_odd, listed, packed, image, k_out, accl, accs),
+        [VMEM] * 9,
+        [vmem(2 * reach, SUBLANES, width), todo, *held],
         aliases={7: 2},
     )
     sums = lax.all_to_all(sums, AXES, 0, 0, tiled=True)

time: 55.4 us -> 52.7 us (0.951); the launches traced: 55.5 us -> 51.9 us
  blocking collectives: 17.9 us -> 14.3 us
  starting transfers between devices: 8.04 us -> 9.45 us
  Pallas kernels: 28.2 us -> 27.4 us
  local copies, waits for them, and re-layouts: 0.65 us -> 0 us
    all_to_all x1, blocking collectives: 17.9 us -> 14.3 us  [local(): sums = lax.all_to_all(sums, AXES, 0, 0, tiled=True)]
    ppermute x4, starting transfers between devices: 8.04 us -> 9.45 us  [swap(): return lax.ppermute(value, AXES, pairs + [(b, a) for a, b in pairs])]
    pallas_call x6, Pallas kernels: 28.2 us -> 27.4 us  [call(): pl.pallas_call(kernel, out_shape=out_shape, in_specs=specs, out_specs=jax...]
    unnamed x2 -> x0, local copies, waits for them, and re-layouts: 0.65 us -> none
  transfers between devices with their start and end apart: 4 -> 4, of which waited for: 0 -> 0; matrix products, arithmetic and copies ran while one was open for 0% -> 0% of each run, Pallas kernels for 35% -> 37%
where the time goes in v1:
time: 52.7 us; the launch traced here: 51.9 us
  Pallas kernels  27.4 us (52%)
  blocking collectives  14.3 us (27%)
  starting transfers between devices  9.45 us (18%)
  between operations  0.72 us (1%)
    pallas_call x6, Pallas kernels, call(): pl.pallas_call(kernel, out_shape=out_shape, in_specs=specs, out_specs=jax...  27.4 us
    all_to_all x1, blocking collectives, local(): sums = lax.all_to_all(sums, AXES, 0, 0, tiled=True)  14.3 us
    ppermute x4, starting transfers between devices, swap(): return lax.ppermute(value, AXES, pairs + [(b, a) for a, b in pairs])  9.45 us
  transfers between devices with their start and end apart: 4, of which 0 were waited for; matrix products, arithmetic and copies ran while one was open for 0% of the time, Pallas kernels for 37%

profile of v1, /device:TPU:0, one launch (start us, length us, event | category | flops | bytes accessed | tf_op | source)
XLA Modules:
  0.0 51.9 jit_solution(10235288004029866902)
XLA Ops:
  0.6 0.9 %shard_map.59 = (f32[4,24,128]{2,1,0:T(8,128)S(1)}, f32[4,24,128]{2,1,0:T(8,128)S(1)}, f32[4,64,128]{2,1,0:T(8,128)S(1)}, s32[8,128]{1,0:T(8,128)S(1)}) custom-call(s32[8]{0:T(128)} %count_in.1, f32[3,8,512]{2,1,0:T(8,128)} %bitcast.7, f32[8,512]{1,0:T(8,128)} %vector_in.1, f32[8,512]{1,0:T(8,128)} %noise_in.1), custom_call_target="tpu_custom_call" | custom-call | tf_op jit(solution)/shard_map/pallas_call | solution.py:34
  1.5 3.1 %collective-permute-start = (f32[4,24,128]{2,1,0:T(8,128)S(1)}, f32[4,24,128]{2,1,0:T(8,128)S(1)}, u32[]{:S(2)}, u32[]{:S(2)}) collective-permute-start(f32[4,24,128]{2,1,0:T(8,128)S(1)} %get-tuple-element.23), channel_id=1, source_target_pairs={{0,1},{2,3},{4,5},{6,7},{8,9},{10,11},{12,13},{14,15},{1,0},{3,2},... | collective-permute-start | bytes 147464 | tf_op jit(solution)/shard_map/ppermute | solution.py:551
  4.6 0.7 %collective-permute-start.1 = (f32[4,24,128]{2,1,0:T(8,128)S(1)}, f32[4,24,128]{2,1,0:T(8,128)S(1)}, u32[]{:S(2)}, u32[]{:S(2)}) collective-permute-start(f32[4,24,128]{2,1,0:T(8,128)S(1)} %get-tuple-element.24), channel_id=1, source_target_pairs={{1,2},{3,4},{5,6},{7,8},{9,10},{11,12},{13,14},{2,1},{4,3},{6,5},{... | collective-permute-start | bytes 147464 | tf_op jit(solution)/shard_map/ppermute | solution.py:551
  5.3 15.6 %shard_map.60 = (f32[8,512,512]{2,1,0:T(8,128)S(1)}, f32[7,512,512]{2,1,0:T(8,128)S(1)}, f32[11,512,512]{2,1,0:T(8,128)S(1)}, f32[8,512,128]{2,1,0:T(8,128)S(1)}...) custom-call(s32[8,128]{1,0:T(8,128)S(1)} %get-tuple-element.22.counts, ...), custom_call_target="tpu_custom_call" | custom-call | tf_op jit(solution)/shard_map/pallas_call | solution.py:34
  20.9 0.0 collective-permute-done.refs_0_
  20.9 0.0 collective-permute-done.1.refs_1_
  20.9 4.3 %shard_map.61 = (f32[12,512,512]{2,1,0:T(8,128)S(1)}, f32[8,512]{1,0:T(8,128)S(1)}, f32[3,512]{1,0:T(4,128)S(1)}, f32[3,512]{1,0:T(4,128)S(1)}, f32[8,512,128]{2,1,0:T(8,128)S(1)}, /*index=5*/f32[8,128]{1,0:T(8,128)S(1)}) custom-call(s32[8,128]{1,0:T(8,128)S(1)} %get-tuple-element.22.counts, ...), custom_call_target="tpu_custom_call", output_to_operand_aliasing={{4}: (6, {})} | custom-call | tf_op jit(solution)/shard_map/pallas_call | solution.py:34
  25.2 5.1 %collective-permute-start.2 = (f32[3,512]{1,0:T(4,128)S(1)}, f32[3,512]{1,0:T(4,128)S(1)}, u32[]{:S(2)}, u32[]{:S(2)}) collective-permute-start(f32[3,512]{1,0:T(4,128)S(1)} %get-tuple-element.30), channel_id=1, source_target_pairs={{0,1},{2,3},{4,5},{6,7},{8,9},{10,11},{12,13},{14,15},{1,0},{3,2},... | collective-permute-start | bytes 18440 | tf_op jit(solution)/shard_map/ppermute | solution.py:551
  30.3 0.6 %collective-permute-start.3 = (f32[3,512]{1,0:T(4,128)S(1)}, f32[3,512]{1,0:T(4,128)S(1)}, u32[]{:S(2)}, u32[]{:S(2)}) collective-permute-start(f32[3,512]{1,0:T(4,128)S(1)} %get-tuple-element.31), channel_id=1, source_target_pairs={{1,2},{3,4},{5,6},{7,8},{9,10},{11,12},{13,14},{2,1},{4,3},{6,5},{... | collective-permute-start | bytes 18440 | tf_op jit(solution)/shard_map/ppermute | solution.py:551
  30.9 3.6 %shard_map.62 = (f32[8,512,128]{2,1,0:T(8,128)S(1)}, f32[8,8,512]{2,1,0:T(8,128)S(1)}) custom-call(s32[8,128]{1,0:T(8,128)S(1)} %get-tuple-element.22.counts, f32[8,512]{1,0:T(8,128)S(1)} %get-tuple-element.33.refs_0_.refs_4_.image, f32[8,512,512]{2,1,0:T(8,128)S(1)} %get-tuple-element.35.refs_1_, f32[7,512,512]{2,1,0:T(8,128)S(1)} %get-tuple-element.36.refs_2_, ...), custom_call_target="tpu_custom_call" | custom-call | tf_op jit(solution)/shard_map/pallas_call | solution.py:34
  34.6 0.0 collective-permute-done.2.refs_0_
  34.6 0.0 collective-permute-done.3.refs_1_
  34.6 2.0 %shard_map.63 = (f32[8,512]{1,0:T(8,128)S(1)}, f32[16,128]{1,0:T(8,128)S(1)}, f32[8,512,128]{2,1,0:T(8,128)S(1)}) custom-call(s32[8,128]{1,0:T(8,128)S(1)} %get-tuple-element.22.counts, f32[3,512]{1,0:T(4,128)S(1)} %collective-permute-done.2.refs_0_, f32[3,512]{1,0:T(4,128)S(1)} %collective-permute-done.3.refs_1_, ...), custom_call_target="tpu_custom_call", output_to_operand_aliasing={{2}: (7, {})} | custom-call | tf_op jit(solution)/shard_map/pallas_call | solution.py:34
  36.6 14.3 %all_to_all.11 = f32[16,1,128]{2,1,0:T(1,128)S(1)} all-to-all(f32[16,1,128]{2,1,0:T(1,128)S(1)} %bitcast.6), channel_id=1, replica_groups=mesh['runs'=2,'grp'=4,'mem'=4] {'grp','mem'}, dimensions={0} | all-to-all | bytes 16384 | tf_op jit(solution)/shard_map/all_to_all | solution.py:633
  50.9 1.0 %shard_map.64 = (f32[8,512]{1,0:T(8,128)}, f32[8,512]{1,0:T(8,128)}) custom-call(f32[16,128]{1,0:T(8,128)S(1)} %bitcast.5, f32[4,64,128]{2,1,0:T(8,128)S(1)} %get-tuple-element.25.refs_0_.refs_2_.refs_3_.packed, f32[8,512]{1,0:T(8,128)S(1)} %get-tuple-element.33.refs_0_.refs_4_.image, f32[8,512]{1,0:T(8,128)S(1)} %get-tuple-element.41.again), custom_call_target="tpu_custom_call" | custom-call | tf_op jit(solution)/shard_map/pallas_call | solution.py:34
Async XLA Ops:
  1.5 19.4 %collective-permute-start = (f32[4,24,128]{2,1,0:T(8,128)S(1)}, f32[4,24,128]{2,1,0:T(8,128)S(1)}, u32[]{:S(2)}, u32[]{:S(2)}) collective-permute-start(f32[4,24,128]{2,1,0:T(8,128)S(1)} %get-tuple-element.23), channel_id=1, source_target_pairs={{0,1},{2,3},{4,5},{6,7},{8,9},{10,11},{12,13},{14,15},{1,0},{3,2},... | collective-permute-start | bytes 147464 | tf_op jit(solution)/shard_map/ppermute | solution.py:551
  4.6 16.3 %collective-permute-start.1 = (f32[4,24,128]{2,1,0:T(8,128)S(1)}, f32[4,24,128]{2,1,0:T(8,128)S(1)}, u32[]{:S(2)}, u32[]{:S(2)}) collective-permute-start(f32[4,24,128]{2,1,0:T(8,128)S(1)} %get-tuple-element.24), channel_id=1, source_target_pairs={{1,2},{3,4},{5,6},{7,8},{9,10},{11,12},{13,14},{2,1},{4,3},{6,5},{... | collective-permute-start | bytes 147464 | tf_op jit(solution)/shard_map/ppermute | solution.py:551
  25.2 9.4 %collective-permute-start.2 = (f32[3,512]{1,0:T(4,128)S(1)}, f32[3,512]{1,0:T(4,128)S(1)}, u32[]{:S(2)}, u32[]{:S(2)}) collective-permute-start(f32[3,512]{1,0:T(4,128)S(1)} %get-tuple-element.30), channel_id=1, source_target_pairs={{0,1},{2,3},{4,5},{6,7},{8,9},{10,11},{12,13},{14,15},{1,0},{3,2},... | collective-permute-start | bytes 18440 | tf_op jit(solution)/shard_map/ppermute | solution.py:551
  30.3 4.3 %collective-permute-start.3 = (f32[3,512]{1,0:T(4,128)S(1)}, f32[3,512]{1,0:T(4,128)S(1)}, u32[]{:S(2)}, u32[]{:S(2)}) collective-permute-start(f32[3,512]{1,0:T(4,128)S(1)} %get-tuple-element.31), channel_id=1, source_target_pairs={{1,2},{3,4},{5,6},{7,8},{9,10},{11,12},{13,14},{2,1},{4,3},{6,5},{... | collective-permute-start | bytes 18440 | tf_op jit(solution)/shard_map/ppermute | solution.py:551
